TPU v7x, 32 devices: a whole 2x2x4 slice. The times are simulated.
32 devices in a mesh: sub: 4 (over y, x), beam: 8 (over z, core).
Axes of the slice: x: 2, y: 2, z: 4, core: 2. Of those that a mesh axis runs over, the one named last changes fastest.
Arguments:
- voltages: bfloat16 [1024, 256, 2, 1024], P(('sub', 'beam')), may hold values from -6 to 6
- weights: bfloat16 [256, 2, 1024, 1024], P(('sub', 'beam')), may hold values from -0.1875 to 0.1875
- antenna_map: int32 [1024], replicated, may hold values from 0 to 1023, each once
- delays: int32 [256, 32], P('sub'), may hold values from 0 to 127, as said below
Outputs:
- filterbank: bfloat16 [256, 1024, 256], P('sub', 'beam')
- series: float32 [32, 1024, 128], P('sub', 'beam')
Inputs may be any that keep to these rules, and one draw needn't show every extreme that they name: antenna_map is a permutation of the antennas. delays never rise with the channel and never fall with the trial; trial 0 has no delay.
All inputs are finite; a program needn't handle non-finite values.
Results may differ from a plain program's by a relative error of at most 0.008.
Values may be sent and summed in bfloat16 or wider, within the bound.
A program may use at most 192 MiB of HBM per device.

v0:
```python
import math

import jax
import jax.numpy as jnp
from jax import lax
from jax.sharding import PartitionSpec as P

A = 1024
NFFT = 1024
C = 256
TRIALS = 32
OUT = 128


def dft_table():
    sample = jnp.arange(NFFT, dtype=jnp.int32)
    channel = jnp.arange(C, dtype=jnp.int32)
    turns = channel[:, None] * sample[None, :] % NFFT
    phase = turns.astype(jnp.float32) * (2.0 * math.pi / NFFT)
    cosine = jnp.cos(phase) / math.sqrt(NFFT)
    sine = jnp.sin(phase) / math.sqrt(NFFT)
    real_row = jnp.stack([cosine, sine], axis=1)
    imag_row = jnp.stack([-sine, cosine], axis=1)
    return jnp.stack([real_row, imag_row], axis=0).astype(jnp.bfloat16)


def on_device(voltages, weights, antenna_map, delays):
    antenna_per_device = voltages.shape[0]
    frame_count = voltages.shape[1]
    local_spectra = jnp.einsum(
        "ocin,afin->aocf", dft_table(), voltages, preferred_element_type=jnp.float32
    ).astype(jnp.bfloat16)
    subband_count = lax.axis_size("sub")
    beam_count = lax.axis_size("beam")
    owned_channels = C // (subband_count * beam_count)
    direct_path = local_spectra.reshape(
        1, antenna_per_device, 2, subband_count * beam_count, owned_channels, frame_count
    )
    moved = lax.all_to_all(direct_path, ("sub", "beam"), split_axis=3, concat_axis=0, tiled=True)
    spectra = moved.reshape(A, 2, owned_channels, frame_count)
    inverse = jnp.zeros((A,), jnp.int32).at[antenna_map].set(jnp.arange(A, dtype=jnp.int32))
    by_antenna = jnp.take(spectra, inverse, axis=0)
    products = jnp.einsum(
        "cjba,aicf->cjibf", weights, by_antenna, preferred_element_type=jnp.float32
    )
    beam_re = products[:, 0, 0] - products[:, 1, 1]
    beam_im = products[:, 0, 1] + products[:, 1, 0]
    power = (beam_re * beam_re + beam_im * beam_im).astype(jnp.bfloat16)
    filterbank = lax.all_to_all(power, "beam", split_axis=1, concat_axis=0, tiled=True)
    sub_channels = filterbank.shape[0]
    beams_here = filterbank.shape[1]
    channel_block = 4
    frame_pos = jnp.arange(frame_count, dtype=jnp.int32)
    out_pos = jnp.arange(OUT, dtype=jnp.int32)

    def add_block(block_index, total):
        start = block_index * channel_block
        spectra_piece = lax.dynamic_slice_in_dim(filterbank, start, channel_block, 0)
        shifts = lax.dynamic_slice_in_dim(delays, start, channel_block, 0)
        channel_selector = (
            frame_pos[None, :, None, None]
            == out_pos[None, None, None, :] + shifts[:, None, :, None]
        ).astype(jnp.bfloat16)
        return total + jnp.einsum(
            "jsv,jvra->rsa", spectra_piece, channel_selector, preferred_element_type=jnp.float32
        )

    start_total = jnp.zeros((TRIALS, beams_here, OUT), jnp.float32)
    total = lax.fori_loop(0, sub_channels // channel_block, add_block, start_total)
    series = lax.psum_scatter(
        (total * (1.0 / C)).astype(jnp.bfloat16), "sub", scatter_dimension=0, tiled=True
    ).astype(jnp.float32)
    return (filterbank, series)


def solution(mesh):
    placed = (
        P(("sub", "beam"), None, None, None),
        P(("sub", "beam"), None, None, None),
        P(),
        P("sub", None),
    )
    return jax.shard_map(
        on_device,
        mesh=mesh,
        in_specs=placed,
        out_specs=(P("sub", "beam", None), P("sub", "beam", None)),
        check_vma=False,
    )
```

profile of v0, /device:TPU:0, one launch (start us, length us, event | category | flops | bytes accessed | tf_op | source)
XLA Modules:
  0.0 576.4 jit_solution(14343754354964209635)
XLA Ops:
  7.2 4.3 negate_convert_fusion
  15.7 32.5 %fusion.17 = bf16[1,32,2,32,8,256]{5,4,3,1,2,0:T(8,128)(2,1)} fusion(bf16[32,256,2,1024]{3,2,1,0:T(2,128)(2,1)} %param.6, bf16[1,256,2,1024]{3,1,2,0:T(8,128)(2,1)S(1)} %get-tuple-element.140, bf16[1,256,2,1024]{3,1,2,0:T(8,128)(2,1)S(1)} %get-tuple-element.139), kind=kOutput, calls=%fused_computation.20 | convolution fusion | flops 17188257792 | bytes 44040192 | tf_op jit(solution)/shard_map/ocin,afin->aocf/dot_general | solution.py:30
  48.2 7.6 %copy.15 = bf16[1,32,2,32,8,256]{5,4,2,1,0,3:T(8,128)(2,1)} copy(bf16[1,32,2,32,8,256]{5,4,3,1,2,0:T(8,128)(2,1)} %fusion.17) | data formatting | bytes 16777216 | tf_op jit(solution)/shard_map/reshape | solution.py:36
  55.8 7.6 %all-to-all-start = ((bf16[1,32,2,32,8,256]{5,4,2,1,0,3:T(8,128)(2,1)}), bf16[1,32,2,32,8,256]{5,4,2,1,0,3:T(8,128)(2,1)}, u32[]{:S(2)}, u32[]{:S(2)}) async-start(bf16[1,32,2,32,8,256]{5,4,2,1,0,3:T(8,128)(2,1)} %copy.15), calls=%async_computation | async-start | bytes 16777216 | tf_op jit(solution)/shard_map/all_to_all | solution.py:39
  63.5 4.3 scatter_custom_fusion
  67.8 180.3 %all-to-all-done = bf16[1,32,2,32,8,256]{5,4,2,1,0,3:T(8,128)(2,1)} async-done(((bf16[1,32,2,32,8,256]{5,4,2,1,0,3:T(8,128)(2,1)}), bf16[1,32,2,32,8,256]{5,4,2,1,0,3:T(8,128)(2,1)}, u32[]{:S(2)}, u32[]{:S(2)}) %all-to-all-start) | async-done | bytes 8388640 | tf_op jit(solution)/shard_map/all_to_all | solution.py:39
  248.2 13.1 %gather_fusion = bf16[1024,2,8,256]{3,2,1,0:T(8,128)(2,1)} fusion(bf16[1024,2,8,256]{3,2,1,0:T(8,128)(2,1)} %bitcast.11, s32[1024]{0:T(1024)S(1)} %fusion.35), kind=kCustom, calls=%fused_computation | custom fusion | bytes 16781312 | tf_op jit(solution)/shard_map/jit(_take)/gather | solution.py:42
  261.2 8.7 %select_bitcast_fusion = bf16[1024,2,8,256,1]{3,2,1,0,4:T(8,128)(2,1)} fusion(bf16[1024,2,8,256]{3,2,1,0:T(8,128)(2,1)} %gather_fusion, pred[1024]{0:T(1024)(128)(4,1)S(1)} %compare_and_fusion), kind=kLoop, calls=%fused_computation.28 | loop fusion | flops 4194304 | bytes 16778240 | tf_op jit(solution)/shard_map/jit(_take)/select_n | solution.py:42
  269.9 73.6 %fusion.14 = f32[8,2,2,1024,256]{3,4,1,2,0:T(8,128)} fusion(bf16[8,2,1024,1024]{3,2,1,0:T(8,128)(2,1)} %param.7, bf16[1024,2,8,256,1]{3,2,1,0,4:T(8,128)(2,1)} %select_bitcast_fusion), kind=kOutput, calls=%fused_computation.19 | convolution fusion | flops 17179869184 | bytes 75497472 | tf_op jit(solution)/shard_map/cjba,aicf->cjibf/dot_general | solution.py:43
  343.5 14.9 %fusion.25 = bf16[8,1024,256]{1,2,0:T(8,128)(2,1)} fusion(f32[8,2,2,1024,256]{3,4,1,2,0:T(8,128)} %fusion.14), kind=kLoop, calls=%fused_computation.29 | loop fusion | flops 12582912 | bytes 37748736 | tf_op jit(solution)/shard_map/convert_element_type | solution.py:48
  358.4 7.0 %copy.17 = bf16[8,1024,256]{2,0,1:T(8,128)(2,1)} copy(bf16[8,1024,256]{1,2,0:T(8,128)(2,1)} %fusion.25) | data formatting | bytes 8388608 | tf_op jit(solution)/shard_map/convert_element_type | solution.py:48
  365.4 4.7 all-to-all-start.1
  370.1 93.9 %all-to-all-done.1 = bf16[8,1024,256]{2,0,1:T(8,128)(2,1)} async-done(((bf16[8,1024,256]{2,0,1:T(8,128)(2,1)}), bf16[8,1024,256]{2,0,1:T(8,128)(2,1)}, u32[]{:S(2)}, u32[]{:S(2)}) %all-to-all-start.1) | async-done | bytes 4194336 | tf_op jit(solution)/shard_map/all_to_all | solution.py:49
  464.1 5.3 copy.18
  469.4 69.0 %while.14 = (s32[]{:T(128)}, f32[32,128,128]{1,2,0:T(8,128)S(1)}, s32[64,32]{0,1:T(8,128)S(1)}, bf16[64,128,256]{2,1,0:T(8,128)(2,1)}, s32[]{:T(128)}, /*index=5*/s32[]{:T(128)}, s32[]{:T(128)}, s32[]{:T(128)}) while((s32[]{:T(128)}, f32[32,128,128]{1,2,0:T(8,128)S(1)}, s32[64,32]{0,1:T(8,128)S(1)}, ...), condition=%wide.region_2.3_spmd.clone, body=%wide.region_1.2_spmd.clone.sunk | while | flops 1079001088 | bytes 4589205 | solution.py:69
  473.9 4.1 bitcast_add_fusion.2
  508.4 4.1 bitcast_add_fusion.2
  512.7 4.1 bitcast_add_fusion.2
  517.0 4.1 bitcast_add_fusion.2
  521.3 4.1 bitcast_add_fusion.2
  525.6 4.1 bitcast_add_fusion.2
  529.9 4.1 bitcast_add_fusion.2
  534.2 4.1 bitcast_add_fusion.2
  542.9 24.9 %reduce-scatter.2.cloned.1.call-done = bf16[8,128,128]{2,1,0:T(8,128)(2,1)} async-done(((bf16[32,128,128]{2,1,0:T(8,128)(2,1)}), bf16[8,128,128]{2,1,0:T(8,128)(2,1)}) %reduce-scatter.2.cloned.1.call-update) | async-done | bytes 262160 | tf_op jit(solution)/shard_map/reduce_scatter | solution.py:70
  (58 shorter events, 46.0 us)
Async XLA Ops:
  55.8 7.6 %copy-start.2 = (s32[1024]{0:T(1024)S(1)}, s32[1024]{0:T(1024)}, u32[]{:S(2)}) copy-start(s32[1024]{0:T(1024)} %param.8) | copy-start | bytes 12292
  55.8 192.3 %all-to-all-start = ((bf16[1,32,2,32,8,256]{5,4,2,1,0,3:T(8,128)(2,1)}), bf16[1,32,2,32,8,256]{5,4,2,1,0,3:T(8,128)(2,1)}, u32[]{:S(2)}, u32[]{:S(2)}) async-start(bf16[1,32,2,32,8,256]{5,4,2,1,0,3:T(8,128)(2,1)} %copy.15), calls=%async_computation | async-start | bytes 16777216 | tf_op jit(solution)/shard_map/all_to_all | solution.py:39
  365.4 104.0 %copy-start.1 = (s32[64,32]{0,1:T(8,128)S(1)}, s32[64,32]{0,1:T(8,128)}, u32[]{:S(2)}) copy-start(s32[64,32]{0,1:T(8,128)} %param.9) | copy-start | bytes 24580
  365.4 98.7 %all-to-all-start.1 = ((bf16[8,1024,256]{2,0,1:T(8,128)(2,1)}), bf16[8,1024,256]{2,0,1:T(8,128)(2,1)}, u32[]{:S(2)}, u32[]{:S(2)}) async-start(bf16[8,1024,256]{2,0,1:T(8,128)(2,1)} %copy.17), calls=%async_computation.1 | async-start | bytes 8388608 | tf_op jit(solution)/shard_map/all_to_all | solution.py:49
  370.1 197.7 %reduce-scatter.2.cloned.1.call-start = ((), (), s32[]{:S(2)}) async-start(), calls=%async_computation.3 | async-start | bytes 1310720 | tf_op jit(solution)/shard_map/reduce_scatter | solution.py:70
  538.4 1.3 copy-start
Sparse Core Ops, SparseCore 0:
  543.0 24.7 reduce-scatter.1
where the time goes:
time: 578 us; the launch traced here: 576 us
  waiting for transfers between devices  299 us (52%)
  matrix products  172 us (30%)
  local copies, waits for them, and re-layouts  41.7 us (7%)
  other arithmetic  36.6 us (6%)
  between operations  14.1 us (2%)
  starting transfers between devices  12.3 us (2%)
    all_to_all x1, waiting for transfers between devices, on_device(): lax.all_to_all(direct_path, ('sub', 'beam'), split_axis=3, concat_axis=0,...  180 us
    all_to_all x1, waiting for transfers between devices, on_device(): lax.all_to_all(power, 'beam', split_axis=1, concat_axis=0, tiled=True)  93.9 us
    dot_general x1, matrix products, on_device(): jnp.einsum('cjba,aicf->cjibf', weights, by_antenna, preferred_element_typ...  73.6 us
    dot_general x16, matrix products, add_block(): jnp.einsum('jsv,jvra->rsa', spectra_piece, channel_selector, preferred_el...  65.5 us
    dot_general x1, matrix products, on_device(): jnp.einsum('ocin,afin->aocf', dft_table(), voltages, preferred_element_ty...  32.5 us
    reduce_scatter x1, waiting for transfers between devices, on_device(): lax.psum_scatter((total * (1.0 / C)).astype(jnp.bfloat16), 'sub', scatter...  24.9 us
    convert_element_type x1, other arithmetic, on_device(): power = (beam_re * beam_re + beam_im * beam_im).astype(jnp.bfloat16)  14.9 us
    gather x1, local copies, waits for them, and re-layouts, on_device(): by_antenna = jnp.take(spectra, inverse, axis=0)  13.1 us
  transfers between devices with their start and end apart: 3, of which 3 were waited for; matrix products, arithmetic and copies ran while one was open for 1% of the time, Pallas kernels for 0%

commit v1 on v0

v1 whole, which is shorter than its diff:
```python
import functools
import math

import jax
import jax.numpy as jnp
import numpy as np
from jax import lax
from jax.experimental import pallas as pl
from jax.experimental.pallas import tpu as pltpu
from jax.sharding import PartitionSpec as P

VMEM_BYTES = 48 * 1024 * 1024


def dft_rows(channels, samples):
    turns = (channels[:, None] * np.arange(samples)[None, :]) % samples
    phase = turns.astype(np.float32) * np.float32(2.0 * math.pi / samples)
    cosine = np.cos(phase) / math.sqrt(samples)
    sine = np.sin(phase) / math.sqrt(samples)
    real_row = np.stack([cosine, sine], axis=1)
    imag_row = np.stack([-sine, cosine], axis=1)
    return jnp.asarray(np.stack([real_row, imag_row], axis=1).astype(np.float32), jnp.bfloat16)


def beam_kernel(map_ref, x_ref, w_ref, out_ref, select, ordered):
    antennas = select.shape[0]
    frames = x_ref.shape[-1]

    @pl.when((pl.program_id(0) == 0) & (pl.program_id(1) == 0))
    def _():
        wanted = lax.broadcasted_iota(jnp.int32, (antennas, antennas), 0)
        select[...] = (wanted == map_ref[...]).astype(jnp.bfloat16)

    @pl.when(pl.program_id(1) == 0)
    def _():
        for part in range(2):
            rows = x_ref[:, 0, part].reshape(antennas, frames)
            ordered[:, part * frames:(part + 1) * frames] = jnp.dot(
                select[...], rows, preferred_element_type=jnp.float32
            ).astype(jnp.bfloat16)

    by_re = jnp.dot(w_ref[0, 0], ordered[...], preferred_element_type=jnp.float32)
    by_im = jnp.dot(w_ref[0, 1], ordered[...], preferred_element_type=jnp.float32)
    beam_re = by_re[:, :frames] - by_im[:, frames:]
    beam_im = by_re[:, frames:] + by_im[:, :frames]
    power = (beam_re * beam_re + beam_im * beam_im).astype(out_ref.dtype)
    out_ref[...] = power.reshape(out_ref.shape)


def form_beams(antenna_map, moved, weights, chunk, beam_count):
    senders, channels, _, local, frames = moved.shape
    antennas = senders * local
    beams = weights.shape[2]
    per_owner = beams // beam_count
    owners_step = max(1, 512 // per_owner)
    rows = owners_step * per_owner
    flops = channels * (2 * antennas * antennas * 2 * frames + 4 * beams * antennas * 2 * frames)
    nbytes = channels * (4 * beams * antennas + 4 * antennas * frames + 2 * beams * frames)
    return pl.pallas_call(
        beam_kernel,
        grid=(channels, beams // rows),
        in_specs=[
            pl.BlockSpec((1, antennas), lambda c, b: (0, 0)),
            pl.BlockSpec((senders, 1, 2, local, frames), lambda c, b: (0, c, 0, 0, 0)),
            pl.BlockSpec((1, 2, rows, antennas), lambda c, b: (chunk * channels + c, 0, b, 0)),
        ],
        out_specs=pl.BlockSpec((owners_step, 1, per_owner, frames), lambda c, b: (b, c, 0, 0)),
        out_shape=jax.ShapeDtypeStruct((beam_count, channels, per_owner, frames), jnp.bfloat16),
        scratch_shapes=[
            pltpu.VMEM((antennas, antennas), jnp.bfloat16),
            pltpu.VMEM((antennas, 2 * frames), jnp.bfloat16),
        ],
        compiler_params=pltpu.CompilerParams(vmem_limit_bytes=VMEM_BYTES),
        cost_estimate=pl.CostEstimate(flops=flops, bytes_accessed=nbytes, transcendentals=0),
        name="form_beams",
    )(antenna_map.reshape(1, antennas), moved, weights)


def dedisperse_kernel(scale, first, delays_ref, x_ref, *refs):
    if first:
        bank_ref, total_ref, turned = refs
        earlier = None
    else:
        earlier, _, bank_ref, total_ref, turned = refs
    senders, channels = x_ref.shape[:2]
    trials, out_frames = total_ref.shape[:2]
    bank_ref[:, 0] = x_ref[...]

    @pl.loop(0, senders)
    def _(sender):
        for channel in range(channels):
            turned[sender * channels + channel] = x_ref[sender, channel].astype(jnp.float32).T

    @pl.loop(0, trials)
    def _(trial):
        total = None if first else earlier[trial]
        for index in range(senders * channels):
            piece = turned[index, pl.ds(delays_ref[index, trial], out_frames), :]
            total = piece if total is None else total + piece
        if scale is not None:
            total = total * scale
        total_ref[trial] = total.astype(total_ref.dtype)


def dedisperse(delays, power, earlier, bank, chunk, chunks, out_frames, scale):
    senders, channels, beams, frames = power.shape
    trials = delays.shape[1]
    first = earlier is None
    whole = lambda: pl.BlockSpec(memory_space=pltpu.VMEM)
    bank_block = pl.BlockSpec((senders, 1, channels, beams, frames), lambda i: (0, chunk, 0, 0, 0))
    operands = [delays, power] + ([] if first else [earlier, bank])
    in_specs = [pl.BlockSpec(memory_space=pltpu.SMEM), whole()]
    if not first:
        in_specs += [whole(), pl.BlockSpec(memory_space=pl.ANY)]
    total_type = jnp.float32 if scale is None else jnp.bfloat16
    work = senders * channels * trials * out_frames * beams
    return pl.pallas_call(
        functools.partial(dedisperse_kernel, scale, first),
        grid=(1,),
        in_specs=in_specs,
        out_specs=[bank_block, whole()],
        out_shape=[
            jax.ShapeDtypeStruct((senders, chunks, channels, beams, frames), jnp.bfloat16),
            jax.ShapeDtypeStruct((trials, out_frames, beams), total_type),
        ],
        scratch_shapes=[pltpu.VMEM((senders * channels, frames, beams), jnp.float32)],
        input_output_aliases={} if first else {3: 0},
        compiler_params=pltpu.CompilerParams(vmem_limit_bytes=VMEM_BYTES),
        cost_estimate=pl.CostEstimate(flops=4 * work, bytes_accessed=4 * 1024 * 1024, transcendentals=0),
        name="dedisperse",
    )(*operands)


def on_device(voltages, weights, antenna_map, delays):
    samples = voltages.shape[3]
    sub_count = lax.axis_size("sub")
    beam_count = lax.axis_size("beam")
    devices = sub_count * beam_count
    owned = weights.shape[0]
    all_channels = owned * devices
    trials = delays.shape[1]
    out_frames = voltages.shape[1] // 2
    chunks = min(4, owned)
    per_chunk = owned // chunks
    first_of = np.arange(devices)[:, None] * owned + np.arange(per_chunk)[None, :]

    bank = total = None
    by_chunk = delays.reshape(beam_count, chunks, per_chunk, trials)
    for chunk in range(chunks):
        table = dft_rows((first_of + chunk * per_chunk).reshape(-1), samples)
        table = table.reshape(devices, per_chunk, 2, 2, samples)
        spectra = jnp.einsum(
            "dcoin,afin->dcoaf", table, voltages, preferred_element_type=jnp.float32
        ).astype(jnp.bfloat16)
        moved = lax.all_to_all(spectra, ("sub", "beam"), split_axis=0, concat_axis=0, tiled=True)
        power = form_beams(antenna_map, moved, weights, chunk, beam_count)
        arrived = lax.all_to_all(power, "beam", split_axis=0, concat_axis=0, tiled=True)
        last = chunk == chunks - 1
        bank, total = dedisperse(
            by_chunk[:, chunk].reshape(beam_count * per_chunk, trials), arrived, total, bank,
            chunk, chunks, out_frames, 1.0 / all_channels if last else None,
        )
    filterbank = bank.reshape(beam_count * owned, bank.shape[3], bank.shape[4])
    parts = total.reshape(sub_count, trials // sub_count, out_frames, bank.shape[3])
    parts = lax.all_to_all(parts, "sub", split_axis=0, concat_axis=0, tiled=True)
    series = jnp.sum(parts.astype(jnp.float32), axis=0).transpose(0, 2, 1)
    return (filterbank, series)


def solution(mesh):
    placed = (
        P(("sub", "beam"), None, None, None),
        P(("sub", "beam"), None, None, None),
        P(),
        P("sub", None),
    )
    return jax.shard_map(
        on_device,
        mesh=mesh,
        in_specs=placed,
        out_specs=(P("sub", "beam", None), P("sub", "beam", None)),
        check_vma=False,
    )
```

time: 578 us -> 395 us (0.68)
  waiting for transfers between devices: 299 us -> 181 us
  matrix products: 172 us -> 84.6 us
  Pallas kernels: 0 us -> 66 us
  other arithmetic: 36.6 us -> 0.16 us
  local copies, waits for them, and re-layouts: 41.7 us -> 12.2 us
  starting transfers between devices: 12.3 us -> 32.6 us
  blocking collectives: 0 us -> 16.6 us
  between operations: 14.1 us -> 0.84 us
    all_to_all x2 -> x8, waiting for transfers between devices: 274 us -> 181 us  [the longest x4 125 us: on_device(): lax.all_to_all(spectra, ('sub', 'beam'), split_axis=0, concat_axis=0, til...]
    dot_general x18 -> x4, matrix products: 172 us -> 84.6 us  [on_device(): jnp.einsum('dcoin,afin->dcoaf', table, voltages, preferred_element_type=j...]
    pallas_call x0 -> x8, Pallas kernels: none -> 66 us  [the longest x4 44.8 us: form_beams(): pl.pallas_call(beam_kernel, grid=(channels, beams // rows), in_specs=[pl....]
    reduce_scatter x1 -> x0, waiting for transfers between devices: 24.9 us -> none  [on_device(): lax.psum_scatter((total * (1.0 / C)).astype(jnp.bfloat16), 'sub', scatter...]
    all_to_all x2 -> x8, starting transfers between devices: 12.3 us -> 32.6 us  [the longest x4 18.1 us: on_device(): lax.all_to_all(spectra, ('sub', 'beam'), split_axis=0, concat_axis=0, til...]
    convert_element_type x3 -> x0, other arithmetic: 17.9 us -> none  [the longest x1 14.9 us: on_device(): power = (beam_re * beam_re + beam_im * beam_im).astype(jnp.bfloat16)]
    all_to_all x0 -> x1, blocking collectives: none -> 16.6 us  [on_device(): lax.all_to_all(parts, 'sub', split_axis=0, concat_axis=0, tiled=True)]
    gather x1 -> x0, local copies, waits for them, and re-layouts: 13.1 us -> none  [on_device(): by_antenna = jnp.take(spectra, inverse, axis=0)]
  transfers between devices with their start and end apart: 3 -> 8, of which waited for: 3 -> 8; matrix products, arithmetic and copies ran while one was open for 1% -> 16% of each run, Pallas kernels for 0% -> 15%
where the time goes in v1:
time: 395 us; the launch traced here: 394 us
  waiting for transfers between devices  181 us (46%)
  matrix products  84.6 us (21%)
  Pallas kernels  66 us (17%)
  starting transfers between devices  32.6 us (8%)
  blocking collectives  16.6 us (4%)
  local copies, waits for them, and re-layouts  12.2 us (3%)
    all_to_all x4, waiting for transfers between devices, on_device(): lax.all_to_all(spectra, ('sub', 'beam'), split_axis=0, concat_axis=0, til...  125 us
    dot_general x4, matrix products, on_device(): jnp.einsum('dcoin,afin->dcoaf', table, voltages, preferred_element_type=j...  84.6 us
    all_to_all x4, waiting for transfers between devices, on_device(): lax.all_to_all(power, 'beam', split_axis=0, concat_axis=0, tiled=True)  55.8 us
    pallas_call x4, Pallas kernels, form_beams(): pl.pallas_call(beam_kernel, grid=(channels, beams // rows), in_specs=[pl....  44.8 us
    pallas_call x4, Pallas kernels, dedisperse(): pl.pallas_call(functools.partial(dedisperse_kernel, scale, first), grid=(...  21.3 us
    all_to_all x4, starting transfers between devices, on_device(): lax.all_to_all(spectra, ('sub', 'beam'), split_axis=0, concat_axis=0, til...  18.1 us
    all_to_all x1, blocking collectives, on_device(): lax.all_to_all(parts, 'sub', split_axis=0, concat_axis=0, tiled=True)  16.6 us
    all_to_all x4, starting transfers between devices, on_device(): lax.all_to_all(power, 'beam', split_axis=0, concat_axis=0, tiled=True)  14.5 us
  transfers between devices with their start and end apart: 8, of which 8 were waited for; matrix products, arithmetic and copies ran while one was open for 16% of the time, Pallas kernels for 15%

profile of v1, /device:TPU:0, one launch (start us, length us, event | category | flops | bytes accessed | tf_op | source)
XLA Modules:
  0.0 394.2 jit_solution(6744916645629608340)
XLA Ops:
  0.6 28.4 %fusion.17 = bf16[32,2,2,32,256]{4,0,3,2,1:T(8,128)(2,1)S(1)} fusion(bf16[32,2,2,2,1024,1]{4,0,3,5,2,1:T(8,128)(2,1)} %constant.22, bf16[32,256,2,1024,1,1]{3,2,1,0,5,4:T(2,128)(2,1)} %bitcast.53), kind=kOutput, calls=%fused_computation.15 | convolution fusion | flops 4294967296 | bytes 36175872 | tf_op jit(solution)/shard_map/dcoin,afin->dcoaf/dot_general | solution.py:152
  31.5 7.5 %all-to-all-start.6 = ((bf16[32,2,2,32,256]{4,3,2,1,0:T(8,128)(2,1)}), bf16[32,2,2,32,256]{4,3,2,1,0:T(8,128)(2,1)S(1)}, u32[]{:S(2)}, u32[]{:S(2)}) async-start(bf16[32,2,2,32,256]{4,3,2,1,0:T(8,128)(2,1)} %copy.84), calls=%async_computation.6 | async-start | bytes 4194304 | tf_op jit(solution)/shard_map/all_to_all | solution.py:155
  39.0 18.7 %fusion.14 = bf16[32,2,2,32,256]{4,0,3,2,1:T(8,128)(2,1)S(1)} fusion(bf16[32,2,2,2,1024,1]{4,0,3,5,2,1:T(8,128)(2,1)S(1)} %copy-done.6, bf16[32,256,2,1024,1,1]{3,2,1,0,5,4:T(2,128)(2,1)} %bitcast.54), kind=kOutput, calls=%fused_computation.14 | convolution fusion | flops 4294967296 | bytes 36175872 | tf_op jit(solution)/shard_map/dcoin,afin->dcoaf/dot_general | solution.py:152
  60.3 28.6 %all-to-all-done.6.x_ref = bf16[32,2,2,32,256]{4,3,2,1,0:T(8,128)(2,1)S(1)} async-done(((bf16[32,2,2,32,256]{4,3,2,1,0:T(8,128)(2,1)}), bf16[32,2,2,32,256]{4,3,2,1,0:T(8,128)(2,1)S(1)}, u32[]{:S(2)}, u32[]{:S(2)}) %all-to-all-start.6) | async-done | bytes 2097184 | tf_op jit(solution)/shard_map/all_to_all | solution.py:155
  92.4 18.7 %fusion.11 = bf16[32,2,2,32,256]{4,0,3,2,1:T(8,128)(2,1)S(1)} fusion(bf16[32,2,2,2,1024,1]{4,0,3,5,2,1:T(8,128)(2,1)S(1)} %copy-done.5, bf16[32,256,2,1024,1,1]{3,2,1,0,5,4:T(2,128)(2,1)} %bitcast.55), kind=kOutput, calls=%fused_computation.13 | convolution fusion | flops 4294967296 | bytes 36175872 | tf_op jit(solution)/shard_map/dcoin,afin->dcoaf/dot_general | solution.py:152
  113.7 28.8 %all-to-all-done.4.x_ref = bf16[32,2,2,32,256]{4,3,2,1,0:T(8,128)(2,1)} async-done(((bf16[32,2,2,32,256]{4,3,2,1,0:T(8,128)(2,1)}), bf16[32,2,2,32,256]{4,3,2,1,0:T(8,128)(2,1)}, u32[]{:S(2)}, u32[]{:S(2)}) %all-to-all-start.4) | async-done | bytes 2097184 | tf_op jit(solution)/shard_map/all_to_all | solution.py:155
  142.5 3.7 all-to-all-start.2
  146.2 18.7 %fusion.8 = bf16[32,2,2,32,256]{4,0,3,2,1:T(8,128)(2,1)S(1)} fusion(bf16[32,2,2,2,1024,1]{4,0,3,5,2,1:T(8,128)(2,1)S(1)} %copy-done.4, bf16[32,256,2,1024,1,1]{3,2,1,0,5,4:T(2,128)(2,1)} %bitcast.56), kind=kOutput, calls=%fused_computation.12 | convolution fusion | flops 4294967296 | bytes 36175872 | tf_op jit(solution)/shard_map/dcoin,afin->dcoaf/dot_general | solution.py:152
  167.5 28.6 %all-to-all-done.2.x_ref = bf16[32,2,2,32,256]{4,3,2,1,0:T(8,128)(2,1)} async-done(((bf16[32,2,2,32,256]{4,3,2,1,0:T(8,128)(2,1)}), bf16[32,2,2,32,256]{4,3,2,1,0:T(8,128)(2,1)}, u32[]{:S(2)}, u32[]{:S(2)}) %all-to-all-start.2) | async-done | bytes 2097184 | tf_op jit(solution)/shard_map/all_to_all | solution.py:155
  199.6 10.8 %form_beams.7 = bf16[8,2,128,256]{3,2,1,0:T(8,128)(2,1)} custom-call(s32[1,1024]{1,0:T(1,128)S(1)} %bitcast.42, bf16[32,2,2,32,256]{4,3,2,1,0:T(8,128)(2,1)S(1)} %all-to-all-done.6.x_ref, bf16[8,2,1024,1024]{3,2,1,0:T(8,128)(2,1)} %w_ref.7), custom_call_target="tpu_custom_call" | custom-call | flops 6442450944 | bytes 11534336 | tf_op jit(solution)/shard_map/form_beams/pallas_call | solution.py:59
  210.3 39.3 %all-to-all-done.x_ref = bf16[32,2,2,32,256]{4,3,2,1,0:T(8,128)(2,1)} async-done(((bf16[32,2,2,32,256]{4,3,2,1,0:T(8,128)(2,1)}), bf16[32,2,2,32,256]{4,3,2,1,0:T(8,128)(2,1)}, u32[]{:S(2)}, u32[]{:S(2)}) %all-to-all-start) | async-done | bytes 2097184 | tf_op jit(solution)/shard_map/all_to_all | solution.py:155
  253.2 11.3 %form_beams.6 = bf16[8,2,128,256]{3,2,1,0:T(8,128)(2,1)} custom-call(s32[1,1024]{1,0:T(1,128)S(1)} %bitcast.43, bf16[32,2,2,32,256]{4,3,2,1,0:T(8,128)(2,1)} %all-to-all-done.4.x_ref, bf16[8,2,1024,1024]{3,2,1,0:T(8,128)(2,1)} %w_ref.7), custom_call_target="tpu_custom_call" | custom-call | flops 6442450944 | bytes 11534336 | tf_op jit(solution)/shard_map/form_beams/pallas_call | solution.py:59
  264.6 15.2 %all-to-all-done.7.x_ref = bf16[8,2,128,256]{3,2,1,0:T(8,128)(2,1)S(1)} async-done(((bf16[8,2,128,256]{3,2,1,0:T(8,128)(2,1)}), bf16[8,2,128,256]{3,2,1,0:T(8,128)(2,1)S(1)}, u32[]{:S(2)}, u32[]{:S(2)}) %all-to-all-start.7) | async-done | bytes 1048608 | tf_op jit(solution)/shard_map/all_to_all | solution.py:157
  283.3 11.3 %form_beams.5 = bf16[8,2,128,256]{3,2,1,0:T(8,128)(2,1)} custom-call(s32[1,1024]{1,0:T(1,128)S(1)} %bitcast.44, bf16[32,2,2,32,256]{4,3,2,1,0:T(8,128)(2,1)} %all-to-all-done.2.x_ref, bf16[8,2,1024,1024]{3,2,1,0:T(8,128)(2,1)} %w_ref.7), custom_call_target="tpu_custom_call" | custom-call | flops 6442450944 | bytes 11534336 | tf_op jit(solution)/shard_map/form_beams/pallas_call | solution.py:59
  294.6 15.2 %all-to-all-done.5.x_ref = bf16[8,2,128,256]{3,2,1,0:T(8,128)(2,1)S(1)} async-done(((bf16[8,2,128,256]{3,2,1,0:T(8,128)(2,1)}), bf16[8,2,128,256]{3,2,1,0:T(8,128)(2,1)S(1)}, u32[]{:S(2)}, u32[]{:S(2)}) %all-to-all-start.5) | async-done | bytes 1048608 | tf_op jit(solution)/shard_map/all_to_all | solution.py:157
  309.8 3.8 all-to-all-start.3
  313.7 11.3 %form_beams.4 = bf16[8,2,128,256]{3,2,1,0:T(8,128)(2,1)} custom-call(s32[1,1024]{1,0:T(1,128)S(1)} %bitcast.45, bf16[32,2,2,32,256]{4,3,2,1,0:T(8,128)(2,1)} %all-to-all-done.x_ref, bf16[8,2,1024,1024]{3,2,1,0:T(8,128)(2,1)} %w_ref.7), custom_call_target="tpu_custom_call" | custom-call | flops 6442450944 | bytes 11534336 | tf_op jit(solution)/shard_map/form_beams/pallas_call | solution.py:59
  325.0 14.9 %all-to-all-done.3.x_ref = bf16[8,2,128,256]{3,2,1,0:T(8,128)(2,1)S(1)} async-done(((bf16[8,2,128,256]{3,2,1,0:T(8,128)(2,1)}), bf16[8,2,128,256]{3,2,1,0:T(8,128)(2,1)S(1)}, u32[]{:S(2)}, u32[]{:S(2)}) %all-to-all-start.3) | async-done | bytes 1048608 | tf_op jit(solution)/shard_map/all_to_all | solution.py:157
  344.6 5.2 %dedisperse.4 = (bf16[8,4,2,128,256]{4,3,2,1,0:T(8,128)(2,1)}, f32[32,128,128]{2,1,0:T(8,128)S(1)}) custom-call(s32[16,32]{1,0:T(8,128)S(1)} %bitcast.46, bf16[8,2,128,256]{3,2,1,0:T(8,128)(2,1)S(1)} %all-to-all-done.7.x_ref), custom_call_target="tpu_custom_call" | custom-call | flops 33554432 | bytes 4194304 | tf_op jit(solution)/shard_map/dedisperse/pallas_call | solution.py:117
  349.8 5.4 %dedisperse.5 = (bf16[8,4,2,128,256]{4,3,2,1,0:T(8,128)(2,1)}, f32[32,128,128]{2,1,0:T(8,128)S(1)}) custom-call(s32[16,32]{1,0:T(8,128)S(1)} %bitcast.49, bf16[8,2,128,256]{3,2,1,0:T(8,128)(2,1)S(1)} %all-to-all-done.5.x_ref, f32[32,128,128]{2,1,0:T(8,128)S(1)} %get-tuple-element.10.refs_0_, ...), custom_call_target="tpu_custom_call", output_to_operand_aliasing={{0}: (3, {})} | custom-call | flops 33554432 | bytes 4194304 | tf_op jit(solution)/shard_map/dedisperse/pallas_call | solution.py:117
  355.1 5.3 %dedisperse.6 = (bf16[8,4,2,128,256]{4,3,2,1,0:T(8,128)(2,1)}, f32[32,128,128]{2,1,0:T(8,128)S(1)}) custom-call(s32[16,32]{1,0:T(8,128)S(1)} %bitcast.48, bf16[8,2,128,256]{3,2,1,0:T(8,128)(2,1)S(1)} %copy-done.1, f32[32,128,128]{2,1,0:T(8,128)S(1)} %get-tuple-element.12.refs_0_, ...), custom_call_target="tpu_custom_call", output_to_operand_aliasing={{0}: (3, {})} | custom-call | flops 33554432 | bytes 4194304 | tf_op jit(solution)/shard_map/dedisperse/pallas_call | solution.py:117
  360.5 10.5 %all-to-all-done.1.x_ref = bf16[8,2,128,256]{3,2,1,0:T(8,128)(2,1)S(1)} async-done(((bf16[8,2,128,256]{3,2,1,0:T(8,128)(2,1)}), bf16[8,2,128,256]{3,2,1,0:T(8,128)(2,1)S(1)}, u32[]{:S(2)}, u32[]{:S(2)}) %all-to-all-start.1) | async-done | bytes 1048608 | tf_op jit(solution)/shard_map/all_to_all | solution.py:157
  371.0 5.4 %dedisperse.7 = (bf16[8,4,2,128,256]{4,3,2,1,0:T(8,128)(2,1)}, bf16[32,128,128]{2,1,0:T(8,128)(2,1)S(1)}) custom-call(s32[16,32]{1,0:T(8,128)S(1)} %bitcast.47, bf16[8,2,128,256]{3,2,1,0:T(8,128)(2,1)S(1)} %all-to-all-done.1.x_ref, f32[32,128,128]{2,1,0:T(8,128)S(1)} %get-tuple-element.14.refs_0_, ...), custom_call_target="tpu_custom_call", output_to_operand_aliasing={{0}: (3, {})} | custom-call | flops 33554432 | bytes 4194304 | tf_op jit(solution)/shard_map/dedisperse/pallas_call | solution.py:117
  376.4 16.6 %all_to_all.45 = bf16[4,8,128,128]{3,2,1,0:T(8,128)(2,1)S(1)} all-to-all(bf16[4,8,128,128]{3,2,1,0:T(8,128)(2,1)S(1)} %bitcast.41), channel_id=1, replica_groups=mesh['sub'=4,'beam'=8] {'sub'}, dimensions={0} | all-to-all | bytes 2097152 | tf_op jit(solution)/shard_map/all_to_all | solution.py:165
  (27 shorter events, 30.0 us)
Async XLA Ops:
  29.0 10.0 %copy-start.6 = (bf16[32,2,2,2,1024,1]{4,0,3,5,2,1:T(8,128)(2,1)S(1)}, bf16[32,2,2,2,1024,1]{4,0,3,5,2,1:T(8,128)(2,1)}, u32[]{:S(2)}) copy-start(bf16[32,2,2,2,1024,1]{4,0,3,5,2,1:T(8,128)(2,1)} %constant.21) | copy-start | bytes 1572868
  31.5 57.4 %all-to-all-start.6 = ((bf16[32,2,2,32,256]{4,3,2,1,0:T(8,128)(2,1)}), bf16[32,2,2,32,256]{4,3,2,1,0:T(8,128)(2,1)S(1)}, u32[]{:S(2)}, u32[]{:S(2)}) async-start(bf16[32,2,2,32,256]{4,3,2,1,0:T(8,128)(2,1)} %copy.84), calls=%async_computation.6 | async-start | bytes 4194304 | tf_op jit(solution)/shard_map/all_to_all | solution.py:155
  57.8 34.7 %copy-start.5 = (bf16[32,2,2,2,1024,1]{4,0,3,5,2,1:T(8,128)(2,1)S(1)}, bf16[32,2,2,2,1024,1]{4,0,3,5,2,1:T(8,128)(2,1)}, u32[]{:S(2)}) copy-start(bf16[32,2,2,2,1024,1]{4,0,3,5,2,1:T(8,128)(2,1)} %constant.20) | copy-start | bytes 1572868
  88.9 53.6 %all-to-all-start.4 = ((bf16[32,2,2,32,256]{4,3,2,1,0:T(8,128)(2,1)}), bf16[32,2,2,32,256]{4,3,2,1,0:T(8,128)(2,1)}, u32[]{:S(2)}, u32[]{:S(2)}) async-start(bf16[32,2,2,32,256]{4,3,2,1,0:T(8,128)(2,1)} %copy.85), calls=%async_computation.4 | async-start | bytes 4194304 | tf_op jit(solution)/shard_map/all_to_all | solution.py:155
  111.2 35.0 %copy-start.4 = (bf16[32,2,2,2,1024,1]{4,0,3,5,2,1:T(8,128)(2,1)S(1)}, bf16[32,2,2,2,1024,1]{4,0,3,5,2,1:T(8,128)(2,1)}, u32[]{:S(2)}) copy-start(bf16[32,2,2,2,1024,1]{4,0,3,5,2,1:T(8,128)(2,1)} %constant.19) | copy-start | bytes 1572868
  142.5 53.6 %all-to-all-start.2 = ((bf16[32,2,2,32,256]{4,3,2,1,0:T(8,128)(2,1)}), bf16[32,2,2,32,256]{4,3,2,1,0:T(8,128)(2,1)}, u32[]{:S(2)}, u32[]{:S(2)}) async-start(bf16[32,2,2,32,256]{4,3,2,1,0:T(8,128)(2,1)} %copy.86), calls=%async_computation.2 | async-start | bytes 4194304 | tf_op jit(solution)/shard_map/all_to_all | solution.py:155
  165.0 34.6 %copy-start.2 = (s32[1024]{0:T(1024)S(1)}, s32[1024]{0:T(1024)}, u32[]{:S(2)}) copy-start(s32[1024]{0:T(1024)} %param.10) | copy-start | bytes 12292
  196.1 53.6 %all-to-all-start = ((bf16[32,2,2,32,256]{4,3,2,1,0:T(8,128)(2,1)}), bf16[32,2,2,32,256]{4,3,2,1,0:T(8,128)(2,1)}, u32[]{:S(2)}, u32[]{:S(2)}) async-start(bf16[32,2,2,32,256]{4,3,2,1,0:T(8,128)(2,1)} %copy.87), calls=%async_computation | async-start | bytes 4194304 | tf_op jit(solution)/shard_map/all_to_all | solution.py:155
  249.7 30.1 %all-to-all-start.7 = ((bf16[8,2,128,256]{3,2,1,0:T(8,128)(2,1)}), bf16[8,2,128,256]{3,2,1,0:T(8,128)(2,1)S(1)}, u32[]{:S(2)}, u32[]{:S(2)}) async-start(bf16[8,2,128,256]{3,2,1,0:T(8,128)(2,1)} %form_beams.7), calls=%async_computation.7 | async-start | bytes 2097152 | tf_op jit(solution)/shard_map/all_to_all | solution.py:157
  279.7 30.1 %all-to-all-start.5 = ((bf16[8,2,128,256]{3,2,1,0:T(8,128)(2,1)}), bf16[8,2,128,256]{3,2,1,0:T(8,128)(2,1)S(1)}, u32[]{:S(2)}, u32[]{:S(2)}) async-start(bf16[8,2,128,256]{3,2,1,0:T(8,128)(2,1)} %form_beams.6), calls=%async_computation.5 | async-start | bytes 2097152 | tf_op jit(solution)/shard_map/all_to_all | solution.py:157
  309.8 30.1 %all-to-all-start.3 = ((bf16[8,2,128,256]{3,2,1,0:T(8,128)(2,1)}), bf16[8,2,128,256]{3,2,1,0:T(8,128)(2,1)S(1)}, u32[]{:S(2)}, u32[]{:S(2)}) async-start(bf16[8,2,128,256]{3,2,1,0:T(8,128)(2,1)} %form_beams.5), calls=%async_computation.3 | async-start | bytes 2097152 | tf_op jit(solution)/shard_map/all_to_all | solution.py:157
  313.6 30.8 %copy-start.3 = (s32[64,32]{0,1:T(8,128)S(1)}, s32[64,32]{0,1:T(8,128)}, u32[]{:S(2)}) copy-start(s32[64,32]{0,1:T(8,128)} %param.11) | copy-start | bytes 24580
  339.9 1.0 copy-start
  340.9 30.1 %all-to-all-start.1 = ((bf16[8,2,128,256]{3,2,1,0:T(8,128)(2,1)}), bf16[8,2,128,256]{3,2,1,0:T(8,128)(2,1)S(1)}, u32[]{:S(2)}, u32[]{:S(2)}) async-start(bf16[8,2,128,256]{3,2,1,0:T(8,128)(2,1)} %form_beams.4), calls=%async_computation.1 | async-start | bytes 2097152 | tf_op jit(solution)/shard_map/all_to_all | solution.py:157
  344.6 10.5 %copy-start.1 = (bf16[8,2,128,256]{3,2,1,0:T(8,128)(2,1)S(1)}, bf16[8,2,128,256]{3,2,1,0:T(8,128)(2,1)}, u32[]{:S(2)}) copy-start(bf16[8,2,128,256]{3,2,1,0:T(8,128)(2,1)} %copy-done) | copy-start | bytes 3145732

commit v2 on v1

--- a/solution.py
+++ b/solution.py
@@ -52,7 +52,7 @@
     antennas = senders * local
     beams = weights.shape[2]
     per_owner = beams // beam_count
-    owners_step = max(1, 512 // per_owner)
+    owners_step = min(beam_count, max(1, 512 // per_owner))
     rows = owners_step * per_owner
     flops = channels * (2 * antennas * antennas * 2 * frames + 4 * beams * antennas * 2 * frames)
     nbytes = channels * (4 * beams * antennas + 4 * antennas * frames + 2 * beams * frames)
@@ -76,7 +76,7 @@
     )(antenna_map.reshape(1, antennas), moved, weights)
 
 
-def dedisperse_kernel(scale, first, delays_ref, x_ref, *refs):
+def dedisperse_kernel(first, delays_ref, x_ref, *refs):
     if first:
         bank_ref, total_ref, turned = refs
         earlier = None
@@ -97,12 +97,10 @@
         for index in range(senders * channels):
             piece = turned[index, pl.ds(delays_ref[index, trial], out_frames), :]
             total = piece if total is None else total + piece
-        if scale is not None:
-            total = total * scale
-        total_ref[trial] = total.astype(total_ref.dtype)
-
-
-def dedisperse(delays, power, earlier, bank, chunk, chunks, out_frames, scale):
+        total_ref[trial] = total
+
+
+def dedisperse(delays, power, earlier, bank, chunk, chunks, out_frames):
     senders, channels, beams, frames = power.shape
     trials = delays.shape[1]
     first = earlier is None
@@ -112,16 +110,15 @@
     in_specs = [pl.BlockSpec(memory_space=pltpu.SMEM), whole()]
     if not first:
         in_specs += [whole(), pl.BlockSpec(memory_space=pl.ANY)]
-    total_type = jnp.float32 if scale is None else jnp.bfloat16
     work = senders * channels * trials * out_frames * beams
     return pl.pallas_call(
-        functools.partial(dedisperse_kernel, scale, first),
+        functools.partial(dedisperse_kernel, first),
         grid=(1,),
         in_specs=in_specs,
         out_specs=[bank_block, whole()],
         out_shape=[
             jax.ShapeDtypeStruct((senders, chunks, channels, beams, frames), jnp.bfloat16),
-            jax.ShapeDtypeStruct((trials, out_frames, beams), total_type),
+            jax.ShapeDtypeStruct((trials, out_frames, beams), jnp.float32),
         ],
         scratch_shapes=[pltpu.VMEM((senders * channels, frames, beams), jnp.float32)],
         input_output_aliases={} if first else {3: 0},
@@ -129,6 +126,90 @@
         cost_estimate=pl.CostEstimate(flops=4 * work, bytes_accessed=4 * 1024 * 1024, transcendentals=0),
         name="dedisperse",
     )(*operands)
+
+
+def finish_kernel(scale, devices, delays_ref, x_ref, earlier, out_ref, turned, own, outgoing, incoming, sent, received):
+    senders, channels = x_ref.shape[:2]
+    share, out_frames = own.shape[:2]
+    me = lax.axis_index("sub")
+    barrier = pltpu.get_barrier_semaphore()
+    for step in range(1, devices):
+        pl.semaphore_signal(
+            barrier, inc=1, device_id={"sub": lax.rem(me + step, devices)}, device_id_type=pl.DeviceIdType.MESH
+        )
+
+    @pl.loop(0, senders)
+    def _(sender):
+        for channel in range(channels):
+            turned[sender * channels + channel] = x_ref[sender, channel].astype(jnp.float32).T
+
+    def total_of(trial):
+        total = earlier[trial]
+        for index in range(senders * channels):
+            total = total + turned[index, pl.ds(delays_ref[index, trial], out_frames), :]
+        return total * scale
+
+    pl.semaphore_wait(barrier, devices - 1)
+    copies = []
+    for step in range(1, devices):
+        peer = lax.rem(me + step, devices)
+
+        @pl.loop(0, share)
+        def _(trial):
+            outgoing[step - 1, trial] = total_of(peer * share + trial).astype(outgoing.dtype)
+
+        copy = pltpu.make_async_remote_copy(
+            src_ref=outgoing.at[step - 1],
+            dst_ref=incoming.at[step - 1],
+            send_sem=sent.at[step - 1],
+            recv_sem=received.at[step - 1],
+            device_id={"sub": peer},
+            device_id_type=pl.DeviceIdType.MESH,
+        )
+        copy.start()
+        copies.append(copy)
+
+    @pl.loop(0, share)
+    def _(trial):
+        own[trial] = total_of(me * share + trial)
+
+    for copy in copies:
+        copy.wait()
+
+    @pl.loop(0, share)
+    def _(trial):
+        total = own[trial]
+        for step in range(devices - 1):
+            total = total + incoming[step, trial].astype(jnp.float32)
+        out_ref[trial] = total.T
+
+
+def finish(delays, power, earlier, scale):
+    senders, channels, beams, frames = power.shape
+    trials, out_frames = earlier.shape[:2]
+    devices = lax.axis_size("sub")
+    share = trials // devices
+    in_vmem = pl.BlockSpec(memory_space=pltpu.VMEM)
+    work = senders * channels * trials * out_frames * beams
+    return pl.pallas_call(
+        functools.partial(finish_kernel, scale, devices),
+        in_specs=[pl.BlockSpec(memory_space=pltpu.SMEM), in_vmem, in_vmem],
+        out_specs=in_vmem,
+        out_shape=jax.ShapeDtypeStruct((share, beams, out_frames), jnp.float32),
+        scratch_shapes=[
+            pltpu.VMEM((senders * channels, frames, beams), jnp.float32),
+            pltpu.VMEM((share, out_frames, beams), jnp.float32),
+            pltpu.VMEM((devices - 1, share, out_frames, beams), jnp.bfloat16),
+            pltpu.VMEM((devices - 1, share, out_frames, beams), jnp.bfloat16),
+            pltpu.SemaphoreType.DMA((devices - 1,)),
+            pltpu.SemaphoreType.DMA((devices - 1,)),
+        ],
+        compiler_params=pltpu.CompilerParams(
+            vmem_limit_bytes=VMEM_BYTES, collective_id=0, has_side_effects=True
+        ),
+        cost_estimate=pl.CostEstimate(flops=4 * work, bytes_accessed=4 * 1024 * 1024, transcendentals=0),
+        name="finish_series",
+    )(delays, power, earlier)
 
 
 def on_device(voltages, weights, antenna_map, delays):
@@ -140,7 +221,7 @@
     all_channels = owned * devices
     trials = delays.shape[1]
     out_frames = voltages.shape[1] // 2
-    chunks = min(4, owned)
+    chunks = min(2, owned)
     per_chunk = owned // chunks
     first_of = np.arange(devices)[:, None] * owned + np.arange(per_chunk)[None, :]
 
@@ -155,15 +236,13 @@
         moved = lax.all_to_all(spectra, ("sub", "beam"), split_axis=0, concat_axis=0, tiled=True)
         power = form_beams(antenna_map, moved, weights, chunk, beam_count)
         arrived = lax.all_to_all(power, "beam", split_axis=0, concat_axis=0, tiled=True)
-        last = chunk == chunks - 1
-        bank, total = dedisperse(
-            by_chunk[:, chunk].reshape(beam_count * per_chunk, trials), arrived, total, bank,
-            chunk, chunks, out_frames, 1.0 / all_channels if last else None,
-        )
+        shifts = by_chunk[:, chunk].reshape(beam_count * per_chunk, trials)
+        if chunk < chunks - 1:
+            bank, total = dedisperse(shifts, arrived, total, bank, chunk, chunks, out_frames)
+        else:
+            bank = lax.dynamic_update_slice(bank, arrived[:, None], (0, chunk, 0, 0, 0))
+            series = finish(shifts, arrived, total, 1.0 / all_channels)
     filterbank = bank.reshape(beam_count * owned, bank.shape[3], bank.shape[4])
-    parts = total.reshape(sub_count, trials // sub_count, out_frames, bank.shape[3])
-    parts = lax.all_to_all(parts, "sub", split_axis=0, concat_axis=0, tiled=True)
-    series = jnp.sum(parts.astype(jnp.float32), axis=0).transpose(0, 2, 1)
     return (filterbank, series)
 
 

time: 395 us -> 366 us (0.927)
  matrix products: 84.6 us -> 59.3 us
  waiting for transfers between devices: 181 us -> 199 us
  blocking collectives: 16.6 us -> 0 us
  starting transfers between devices: 32.6 us -> 18.6 us
  local copies, waits for them, and re-layouts: 12.2 us -> 23.9 us
    dot_general x4 -> x2, matrix products: 84.6 us -> 59.3 us  [on_device(): jnp.einsum('dcoin,afin->dcoaf', table, voltages, preferred_element_type=j...]
    all_to_all x1 -> x0, blocking collectives: 16.6 us -> none  [on_device(): lax.all_to_all(parts, 'sub', split_axis=0, concat_axis=0, tiled=True)]
    all_to_all x4 -> x2, waiting for transfers between devices: 55.8 us -> 65.8 us  [on_device(): lax.all_to_all(power, 'beam', split_axis=0, concat_axis=0, tiled=True)]
    unnamed x16 -> x24, local copies, waits for them, and re-layouts: 2.12 us -> 10.7 us
    all_to_all x4 -> x2, waiting for transfers between devices: 125 us -> 133 us  [on_device(): lax.all_to_all(spectra, ('sub', 'beam'), split_axis=0, concat_axis=0, til...]
    all_to_all x4 -> x2, starting transfers between devices: 14.5 us -> 7.21 us  [on_device(): lax.all_to_all(power, 'beam', split_axis=0, concat_axis=0, tiled=True)]
    all_to_all x4 -> x2, starting transfers between devices: 18.1 us -> 11.4 us  [on_device(): lax.all_to_all(spectra, ('sub', 'beam'), split_axis=0, concat_axis=0, til...]
    pallas_call x4 -> x2, Pallas kernels: 44.8 us -> 39 us  [form_beams(): pl.pallas_call(beam_kernel, grid=(channels, beams // rows), in_specs=[pl....]
  transfers between devices with their start and end apart: 8 -> 4, of which waited for: 8 -> 4; matrix products, arithmetic and copies ran while one was open for 16% -> 10% of each run, Pallas kernels for 15% -> 13%
where the time goes in v2:
time: 366 us
  waiting for transfers between devices  199 us (54%)
  Pallas kernels  64.4 us (18%)
  matrix products  59.3 us (16%)
  local copies, waits for them, and re-layouts  23.9 us (7%)
  starting transfers between devices  18.6 us (5%)
    all_to_all x2, waiting for transfers between devices, on_device(): lax.all_to_all(spectra, ('sub', 'beam'), split_axis=0, concat_axis=0, til...  133 us
    all_to_all x2, waiting for transfers between devices, on_device(): lax.all_to_all(power, 'beam', split_axis=0, concat_axis=0, tiled=True)  65.8 us
    dot_general x2, matrix products, on_device(): jnp.einsum('dcoin,afin->dcoaf', table, voltages, preferred_element_type=j...  59.3 us
    pallas_call x2, Pallas kernels, form_beams(): pl.pallas_call(beam_kernel, grid=(channels, beams // rows), in_specs=[pl....  39 us
    pallas_call x1, Pallas kernels, finish(): pl.pallas_call(functools.partial(finish_kernel, scale, devices), in_specs...  17.1 us
    dot_general x2, local copies, waits for them, and re-layouts, on_device(): jnp.einsum('dcoin,afin->dcoaf', table, voltages, preferred_element_type=j...  13.1 us
    all_to_all x2, starting transfers between devices, on_device(): lax.all_to_all(spectra, ('sub', 'beam'), split_axis=0, concat_axis=0, til...  11.4 us
    unnamed x24, local copies, waits for them, and re-layouts  10.7 us
  transfers between devices with their start and end apart: 4, of which 4 were waited for; matrix products, arithmetic and copies ran while one was open for 10% of the time, Pallas kernels for 13%

profile of v2, /device:TPU:0, one launch (start us, length us, event | category | flops | bytes accessed | tf_op | source)
XLA Modules:
  0.0 365.7 jit_solution(9482462152512638451)
XLA Ops:
  0.6 29.8 %fusion.4 = bf16[32,4,2,32,256]{4,0,3,2,1:T(8,128)(2,1)} fusion(bf16[32,4,2,2,1024,1]{4,0,3,5,2,1:T(8,128)(2,1)} %constant.13, bf16[32,256,2,1024,1,1]{3,2,1,0,5,4:T(2,128)(2,1)} %bitcast.30), kind=kOutput, calls=%fused_computation.6 | convolution fusion | flops 8589934592 | bytes 38797312 | tf_op jit(solution)/shard_map/dcoin,afin->dcoaf/dot_general | solution.py:233
  30.4 6.5 %copy.42 = bf16[32,4,2,32,256]{4,3,2,1,0:T(8,128)(2,1)} copy(bf16[32,4,2,32,256]{4,0,3,2,1:T(8,128)(2,1)} %fusion.4) | data formatting | bytes 8388608 | tf_op jit(solution)/shard_map/dcoin,afin->dcoaf/dot_general | solution.py:233
  36.9 7.6 %all-to-all-start = ((bf16[32,4,2,32,256]{4,3,2,1,0:T(8,128)(2,1)}), bf16[32,4,2,32,256]{4,3,2,1,0:T(8,128)(2,1)}, u32[]{:S(2)}, u32[]{:S(2)}) async-start(bf16[32,4,2,32,256]{4,3,2,1,0:T(8,128)(2,1)} %copy.42), calls=%async_computation | async-start | bytes 8388608 | tf_op jit(solution)/shard_map/all_to_all | solution.py:236
  44.6 29.6 %fusion.7 = bf16[32,4,2,32,256]{4,0,3,2,1:T(8,128)(2,1)} fusion(bf16[32,4,2,2,1024,1]{4,0,3,5,2,1:T(8,128)(2,1)S(1)} %copy-done.10, bf16[32,256,2,1024,1,1]{3,2,1,0,5,4:T(2,128)(2,1)} %bitcast.31), kind=kOutput, calls=%fused_computation.7 | convolution fusion | flops 8589934592 | bytes 38797312 | tf_op jit(solution)/shard_map/dcoin,afin->dcoaf/dot_general | solution.py:233
  74.1 6.5 %copy.41 = bf16[32,4,2,32,256]{4,3,2,1,0:T(8,128)(2,1)} copy(bf16[32,4,2,32,256]{4,0,3,2,1:T(8,128)(2,1)} %fusion.7) | data formatting | bytes 8388608 | tf_op jit(solution)/shard_map/dcoin,afin->dcoaf/dot_general | solution.py:233
  80.7 58.8 %all-to-all-done.x_ref = bf16[32,4,2,32,256]{4,3,2,1,0:T(8,128)(2,1)} async-done(((bf16[32,4,2,32,256]{4,3,2,1,0:T(8,128)(2,1)}), bf16[32,4,2,32,256]{4,3,2,1,0:T(8,128)(2,1)}, u32[]{:S(2)}, u32[]{:S(2)}) %all-to-all-start) | async-done | bytes 4194336 | tf_op jit(solution)/shard_map/all_to_all | solution.py:236
  139.4 3.8 %all-to-all-start.2 = ((bf16[32,4,2,32,256]{4,3,2,1,0:T(8,128)(2,1)}), bf16[32,4,2,32,256]{4,3,2,1,0:T(8,128)(2,1)}, u32[]{:S(2)}, u32[]{:S(2)}) async-start(bf16[32,4,2,32,256]{4,3,2,1,0:T(8,128)(2,1)} %copy.41), calls=%async_computation.2 | async-start | bytes 8388608 | tf_op jit(solution)/shard_map/all_to_all | solution.py:236
  143.3 19.5 %form_beams.2 = bf16[8,4,128,256]{3,2,1,0:T(8,128)(2,1)S(1)} custom-call(s32[1,1024]{1,0:T(1,128)S(1)} %bitcast.27, bf16[32,4,2,32,256]{4,3,2,1,0:T(8,128)(2,1)} %all-to-all-done.x_ref, bf16[8,2,1024,1024]{3,2,1,0:T(8,128)(2,1)} %w_ref.3), custom_call_target="tpu_custom_call" | custom-call | flops 12884901888 | bytes 23068672 | tf_op jit(solution)/shard_map/form_beams/pallas_call | solution.py:59
  162.8 1.3 copy-done.3
  164.1 74.0 %all-to-all-done.2.x_ref = bf16[32,4,2,32,256]{4,3,2,1,0:T(8,128)(2,1)} async-done(((bf16[32,4,2,32,256]{4,3,2,1,0:T(8,128)(2,1)}), bf16[32,4,2,32,256]{4,3,2,1,0:T(8,128)(2,1)}, u32[]{:S(2)}, u32[]{:S(2)}) %all-to-all-start.2) | async-done | bytes 4194336 | tf_op jit(solution)/shard_map/all_to_all | solution.py:236
  238.1 3.6 all-to-all-start.1
  241.7 19.5 %form_beams.3 = bf16[8,4,128,256]{3,2,1,0:T(8,128)(2,1)S(1)} custom-call(s32[1,1024]{1,0:T(1,128)S(1)} %bitcast.28, bf16[32,4,2,32,256]{4,3,2,1,0:T(8,128)(2,1)} %all-to-all-done.2.x_ref, bf16[8,2,1024,1024]{3,2,1,0:T(8,128)(2,1)} %w_ref.3), custom_call_target="tpu_custom_call" | custom-call | flops 12884901888 | bytes 23068672 | tf_op jit(solution)/shard_map/form_beams/pallas_call | solution.py:59
  261.2 1.3 copy-done.2
  262.6 28.1 %all-to-all-done.1.x_ref = bf16[8,4,128,256]{3,2,1,0:T(8,128)(2,1)S(1)} async-done(((bf16[8,4,128,256]{3,2,1,0:T(8,128)(2,1)}), bf16[8,4,128,256]{3,2,1,0:T(8,128)(2,1)S(1)}, u32[]{:S(2)}, u32[]{:S(2)}) %all-to-all-start.1) | async-done | bytes 2097184 | tf_op jit(solution)/shard_map/all_to_all | solution.py:238
  290.7 1.3 copy-done
  292.0 3.6 all-to-all-start.3
  295.7 1.6 copy-done.1
  297.3 8.3 %dedisperse.1 = (bf16[8,2,4,128,256]{4,3,2,1,0:T(8,128)(2,1)}, f32[32,128,128]{2,1,0:T(8,128)S(1)}) custom-call(s32[32,32]{1,0:T(8,128)S(1)} %bitcast.26, bf16[8,4,128,256]{3,2,1,0:T(8,128)(2,1)S(1)} %copy-done.1), custom_call_target="tpu_custom_call" | custom-call | flops 67108864 | bytes 4194304 | tf_op jit(solution)/shard_map/dedisperse/pallas_call | solution.py:114
  305.6 1.3 copy-done.4
  306.9 37.7 %all-to-all-done.3.x_ref = bf16[8,4,128,256]{3,2,1,0:T(8,128)(2,1)S(1)} async-done(((bf16[8,4,128,256]{3,2,1,0:T(8,128)(2,1)}), bf16[8,4,128,256]{3,2,1,0:T(8,128)(2,1)S(1)}, u32[]{:S(2)}, u32[]{:S(2)}) %all-to-all-start.3) | async-done | bytes 2097184 | tf_op jit(solution)/shard_map/all_to_all | solution.py:238
  344.6 1.6 copy-done.5
  346.2 17.1 %finish_series.1 = f32[8,128,128]{2,1,0:T(8,128)S(1)} custom-call(s32[32,32]{1,0:T(8,128)S(1)} %bitcast.25, bf16[8,4,128,256]{3,2,1,0:T(8,128)(2,1)S(1)} %all-to-all-done.3.x_ref, f32[32,128,128]{2,1,0:T(8,128)S(1)} %copy-done.5), custom_call_target="tpu_custom_call" | custom-call | flops 67108864 | bytes 4194304 | tf_op jit(solution)/shard_map/finish_series/pallas_call | solution.py:194
  363.5 0.8 copy.45
  364.4 1.3 copy-done.9
  (18 shorter events, 0.3 us)
Async XLA Ops:
  36.9 7.6 %copy-start.10 = (bf16[32,4,2,2,1024,1]{4,0,3,5,2,1:T(8,128)(2,1)S(1)}, bf16[32,4,2,2,1024,1]{4,0,3,5,2,1:T(8,128)(2,1)}, u32[]{:S(2)}) copy-start(bf16[32,4,2,2,1024,1]{4,0,3,5,2,1:T(8,128)(2,1)} %constant.14) | copy-start | bytes 3145732
  36.9 102.5 %all-to-all-start = ((bf16[32,4,2,32,256]{4,3,2,1,0:T(8,128)(2,1)}), bf16[32,4,2,32,256]{4,3,2,1,0:T(8,128)(2,1)}, u32[]{:S(2)}, u32[]{:S(2)}) async-start(bf16[32,4,2,32,256]{4,3,2,1,0:T(8,128)(2,1)} %copy.42), calls=%async_computation | async-start | bytes 8388608 | tf_op jit(solution)/shard_map/all_to_all | solution.py:236
  80.7 62.6 %copy-start.6 = (s32[1024]{0:T(1024)S(1)}, s32[1024]{0:T(1024)}, u32[]{:S(2)}) copy-start(s32[1024]{0:T(1024)} %param.8) | copy-start | bytes 12292
  139.4 98.7 %all-to-all-start.2 = ((bf16[32,4,2,32,256]{4,3,2,1,0:T(8,128)(2,1)}), bf16[32,4,2,32,256]{4,3,2,1,0:T(8,128)(2,1)}, u32[]{:S(2)}, u32[]{:S(2)}) async-start(bf16[32,4,2,32,256]{4,3,2,1,0:T(8,128)(2,1)} %copy.41), calls=%async_computation.2 | async-start | bytes 8388608 | tf_op jit(solution)/shard_map/all_to_all | solution.py:236
  162.8 1.3 copy-start.3
  238.1 52.6 %all-to-all-start.1 = ((bf16[8,4,128,256]{3,2,1,0:T(8,128)(2,1)}), bf16[8,4,128,256]{3,2,1,0:T(8,128)(2,1)S(1)}, u32[]{:S(2)}, u32[]{:S(2)}) async-start(bf16[8,4,128,256]{3,2,1,0:T(8,128)(2,1)} %copy-done.3), calls=%async_computation.1 | async-start | bytes 4194304 | tf_op jit(solution)/shard_map/all_to_all | solution.py:238
  261.2 1.3 copy-start.2
  262.6 33.1 %copy-start.7 = (s32[64,32]{0,1:T(8,128)S(1)}, s32[64,32]{0,1:T(8,128)}, u32[]{:S(2)}) copy-start(s32[64,32]{0,1:T(8,128)} %param.9) | copy-start | bytes 24580
  290.7 1.3 copy-start
  292.0 52.6 %all-to-all-start.3 = ((bf16[8,4,128,256]{3,2,1,0:T(8,128)(2,1)}), bf16[8,4,128,256]{3,2,1,0:T(8,128)(2,1)S(1)}, u32[]{:S(2)}, u32[]{:S(2)}) async-start(bf16[8,4,128,256]{3,2,1,0:T(8,128)(2,1)} %copy-done.2), calls=%async_computation.3 | async-start | bytes 4194304 | tf_op jit(solution)/shard_map/all_to_all | solution.py:238
  295.7 1.6 copy-start.1
  305.6 1.3 copy-start.4
  344.6 1.6 copy-start.5
  346.2 17.1 %copy-start.8 = (bf16[8,2,4,128,256]{4,3,2,1,0:T(8,128)(2,1)S(1)}, bf16[8,2,4,128,256]{4,3,2,1,0:T(8,128)(2,1)}, u32[]{:S(2)}) copy-start(bf16[8,2,4,128,256]{4,3,2,1,0:T(8,128)(2,1)} %get-tuple-element.4) | copy-start | bytes 12582916
  363.5 2.2 copy-start.9

commit v3 on v2

--- a/solution.py
+++ b/solution.py
@@ -13,13 +13,14 @@
 
 
 def dft_rows(channels, samples):
-    turns = (channels[:, None] * np.arange(samples)[None, :]) % samples
+    turns = (channels[..., None] * np.arange(samples)) % samples
     phase = turns.astype(np.float32) * np.float32(2.0 * math.pi / samples)
     cosine = np.cos(phase) / math.sqrt(samples)
     sine = np.sin(phase) / math.sqrt(samples)
-    real_row = np.stack([cosine, sine], axis=1)
-    imag_row = np.stack([-sine, cosine], axis=1)
-    return jnp.asarray(np.stack([real_row, imag_row], axis=1).astype(np.float32), jnp.bfloat16)
+    real_row = np.stack([cosine, sine], axis=2)
+    imag_row = np.stack([-sine, cosine], axis=2)
+    table = np.stack([real_row, imag_row], axis=1).astype(np.float32)
+    return jnp.asarray(table.reshape(-1, 2, samples), jnp.bfloat16)
 
 
 def beam_kernel(map_ref, x_ref, w_ref, out_ref, select, ordered):
@@ -228,11 +229,12 @@
     bank = total = None
     by_chunk = delays.reshape(beam_count, chunks, per_chunk, trials)
     for chunk in range(chunks):
-        table = dft_rows((first_of + chunk * per_chunk).reshape(-1), samples)
-        table = table.reshape(devices, per_chunk, 2, 2, samples)
+        table = dft_rows((first_of + chunk * per_chunk).T, samples)
         spectra = jnp.einsum(
-            "dcoin,afin->dcoaf", table, voltages, preferred_element_type=jnp.float32
+            "rin,afin->arf", table, voltages, preferred_element_type=jnp.float32
         ).astype(jnp.bfloat16)
+        spectra = spectra.reshape(spectra.shape[0], per_chunk, 2, devices, spectra.shape[2])
+        spectra = spectra.transpose(3, 1, 2, 0, 4)
         moved = lax.all_to_all(spectra, ("sub", "beam"), split_axis=0, concat_axis=0, tiled=True)
         power = form_beams(antenna_map, moved, weights, chunk, beam_count)
         arrived = lax.all_to_all(power, "beam", split_axis=0, concat_axis=0, tiled=True)

time: 366 us -> 366 us (level)
    reshape x0 -> x2, local copies, waits for them, and re-layouts: none -> 13.1 us  [on_device(): spectra.reshape(spectra.shape[0], per_chunk, 2, devices, spectra.shape[2])]
    dot_general x2 -> x0, local copies, waits for them, and re-layouts: 13.1 us -> none  [on_device(): jnp.einsum('dcoin,afin->dcoaf', table, voltages, preferred_element_type=j...]
where the time goes in v3:
time: 366 us
  waiting for transfers between devices  199 us (54%)
  Pallas kernels  64.5 us (18%)
  matrix products  59.3 us (16%)
  local copies, waits for them, and re-layouts  23.9 us (7%)
  starting transfers between devices  18.8 us (5%)
    all_to_all x2, waiting for transfers between devices, on_device(): lax.all_to_all(spectra, ('sub', 'beam'), split_axis=0, concat_axis=0, til...  133 us
    all_to_all x2, waiting for transfers between devices, on_device(): lax.all_to_all(power, 'beam', split_axis=0, concat_axis=0, tiled=True)  65.7 us
    dot_general x2, matrix products, on_device(): jnp.einsum('rin,afin->arf', table, voltages, preferred_element_type=jnp.f...  59.3 us
    pallas_call x2, Pallas kernels, form_beams(): pl.pallas_call(beam_kernel, grid=(channels, beams // rows), in_specs=[pl....  39 us
    pallas_call x1, Pallas kernels, finish(): pl.pallas_call(functools.partial(finish_kernel, scale, devices), in_specs...  17.2 us
    reshape x2, local copies, waits for them, and re-layouts, on_device(): spectra.reshape(spectra.shape[0], per_chunk, 2, devices, spectra.shape[2])  13.1 us
    all_to_all x2, starting transfers between devices, on_device(): lax.all_to_all(spectra, ('sub', 'beam'), split_axis=0, concat_axis=0, til...  11.6 us
    unnamed x24, local copies, waits for them, and re-layouts  10.7 us
  transfers between devices with their start and end apart: 4, of which 4 were waited for; matrix products, arithmetic and copies ran while one was open for 10% of the time, Pallas kernels for 13%

profile of v3, /device:TPU:0, one launch (start us, length us, event | category | flops | bytes accessed | tf_op | source)
XLA Modules:
  0.0 365.8 jit_solution(6658666176222801670)
XLA Ops:
  0.6 29.8 %bitcast_convert_fusion.1 = bf16[256,32,256]{2,0,1:T(8,128)(2,1)} fusion(bf16[256,2,1024,1]{2,0,1,3:T(8,128)(2,1)} %constant.11, bf16[32,256,2,1024]{3,2,1,0:T(2,128)(2,1)} %param.6), kind=kOutput, calls=%fused_computation.5 | convolution fusion | flops 8592031744 | bytes 38797312 | tf_op jit(solution)/shard_map/rin,afin->arf/dot_general | solution.py:233
  30.4 6.5 %copy.32 = bf16[32,4,2,32,256]{4,0,2,1,3:T(8,128)(2,1)} copy(bf16[32,4,2,32,256]{4,3,2,1,0:T(8,128)(2,1)} %bitcast.37) | data formatting | bytes 8388608 | tf_op jit(solution)/shard_map/reshape | solution.py:236
  36.9 7.6 %all-to-all-start = ((bf16[32,4,2,32,256]{4,3,2,1,0:T(8,128)(2,1)}), bf16[32,4,2,32,256]{4,3,2,1,0:T(8,128)(2,1)}, u32[]{:S(2)}, u32[]{:S(2)}) async-start(bf16[32,4,2,32,256]{4,3,2,1,0:T(8,128)(2,1)} %bitcast.36), calls=%async_computation | async-start | bytes 8388608 | tf_op jit(solution)/shard_map/all_to_all | solution.py:238
  44.6 29.5 %bitcast_convert_fusion = bf16[256,32,256]{2,0,1:T(8,128)(2,1)} fusion(bf16[256,2,1024,1]{2,0,1,3:T(8,128)(2,1)S(1)} %copy-done.10, bf16[32,256,2,1024]{3,2,1,0:T(2,128)(2,1)} %param.6), kind=kOutput, calls=%fused_computation.4 | convolution fusion | flops 8592031744 | bytes 38797312 | tf_op jit(solution)/shard_map/rin,afin->arf/dot_general | solution.py:233
  74.1 6.5 %copy.31 = bf16[32,4,2,32,256]{4,0,2,1,3:T(8,128)(2,1)} copy(bf16[32,4,2,32,256]{4,3,2,1,0:T(8,128)(2,1)} %bitcast.38) | data formatting | bytes 8388608 | tf_op jit(solution)/shard_map/reshape | solution.py:236
  80.6 58.8 %all-to-all-done.x_ref = bf16[32,4,2,32,256]{4,3,2,1,0:T(8,128)(2,1)} async-done(((bf16[32,4,2,32,256]{4,3,2,1,0:T(8,128)(2,1)}), bf16[32,4,2,32,256]{4,3,2,1,0:T(8,128)(2,1)}, u32[]{:S(2)}, u32[]{:S(2)}) %all-to-all-start) | async-done | bytes 4194336 | tf_op jit(solution)/shard_map/all_to_all | solution.py:238
  139.4 3.9 %all-to-all-start.2 = ((bf16[32,4,2,32,256]{4,3,2,1,0:T(8,128)(2,1)}), bf16[32,4,2,32,256]{4,3,2,1,0:T(8,128)(2,1)}, u32[]{:S(2)}, u32[]{:S(2)}) async-start(bf16[32,4,2,32,256]{4,3,2,1,0:T(8,128)(2,1)} %bitcast.35), calls=%async_computation.2 | async-start | bytes 8388608 | tf_op jit(solution)/shard_map/all_to_all | solution.py:238
  143.4 19.5 %form_beams.2 = bf16[8,4,128,256]{3,2,1,0:T(8,128)(2,1)S(1)} custom-call(s32[1,1024]{1,0:T(1,128)S(1)} %bitcast.33, bf16[32,4,2,32,256]{4,3,2,1,0:T(8,128)(2,1)} %all-to-all-done.x_ref, bf16[8,2,1024,1024]{3,2,1,0:T(8,128)(2,1)} %w_ref.3), custom_call_target="tpu_custom_call" | custom-call | flops 12884901888 | bytes 23068672 | tf_op jit(solution)/shard_map/form_beams/pallas_call | solution.py:60
  162.9 1.3 copy-done.3
  164.2 74.0 %all-to-all-done.2.x_ref = bf16[32,4,2,32,256]{4,3,2,1,0:T(8,128)(2,1)} async-done(((bf16[32,4,2,32,256]{4,3,2,1,0:T(8,128)(2,1)}), bf16[32,4,2,32,256]{4,3,2,1,0:T(8,128)(2,1)}, u32[]{:S(2)}, u32[]{:S(2)}) %all-to-all-start.2) | async-done | bytes 4194336 | tf_op jit(solution)/shard_map/all_to_all | solution.py:238
  238.2 3.6 all-to-all-start.1
  241.8 19.5 %form_beams.3 = bf16[8,4,128,256]{3,2,1,0:T(8,128)(2,1)S(1)} custom-call(s32[1,1024]{1,0:T(1,128)S(1)} %bitcast.34, bf16[32,4,2,32,256]{4,3,2,1,0:T(8,128)(2,1)} %all-to-all-done.2.x_ref, bf16[8,2,1024,1024]{3,2,1,0:T(8,128)(2,1)} %w_ref.3), custom_call_target="tpu_custom_call" | custom-call | flops 12884901888 | bytes 23068672 | tf_op jit(solution)/shard_map/form_beams/pallas_call | solution.py:60
  261.4 1.3 copy-done.2
  262.7 28.1 %all-to-all-done.1.x_ref = bf16[8,4,128,256]{3,2,1,0:T(8,128)(2,1)S(1)} async-done(((bf16[8,4,128,256]{3,2,1,0:T(8,128)(2,1)}), bf16[8,4,128,256]{3,2,1,0:T(8,128)(2,1)S(1)}, u32[]{:S(2)}, u32[]{:S(2)}) %all-to-all-start.1) | async-done | bytes 2097184 | tf_op jit(solution)/shard_map/all_to_all | solution.py:240
  290.8 1.3 copy-done
  292.1 3.6 all-to-all-start.3
  295.9 1.6 copy-done.1
  297.5 8.4 %dedisperse.1 = (bf16[8,2,4,128,256]{4,3,2,1,0:T(8,128)(2,1)}, f32[32,128,128]{2,1,0:T(8,128)S(1)}) custom-call(s32[32,32]{1,0:T(8,128)S(1)} %bitcast.32, bf16[8,4,128,256]{3,2,1,0:T(8,128)(2,1)S(1)} %copy-done.1), custom_call_target="tpu_custom_call" | custom-call | flops 67108864 | bytes 4194304 | tf_op jit(solution)/shard_map/dedisperse/pallas_call | solution.py:115
  305.8 1.3 copy-done.4
  307.1 37.6 %all-to-all-done.3.x_ref = bf16[8,4,128,256]{3,2,1,0:T(8,128)(2,1)S(1)} async-done(((bf16[8,4,128,256]{3,2,1,0:T(8,128)(2,1)}), bf16[8,4,128,256]{3,2,1,0:T(8,128)(2,1)S(1)}, u32[]{:S(2)}, u32[]{:S(2)}) %all-to-all-start.3) | async-done | bytes 2097184 | tf_op jit(solution)/shard_map/all_to_all | solution.py:240
  344.7 1.6 copy-done.5
  346.3 17.2 %finish_series.1 = f32[8,128,128]{2,1,0:T(8,128)S(1)} custom-call(s32[32,32]{1,0:T(8,128)S(1)} %bitcast.31, bf16[8,4,128,256]{3,2,1,0:T(8,128)(2,1)S(1)} %all-to-all-done.3.x_ref, f32[32,128,128]{2,1,0:T(8,128)S(1)} %copy-done.5), custom_call_target="tpu_custom_call" | custom-call | flops 67108864 | bytes 4194304 | tf_op jit(solution)/shard_map/finish_series/pallas_call | solution.py:195
  363.7 0.8 copy.35
  364.5 1.3 copy-done.9
  (18 shorter events, 0.3 us)
Async XLA Ops:
  36.9 7.6 %copy-start.10 = (bf16[256,2,1024,1]{2,0,1,3:T(8,128)(2,1)S(1)}, bf16[256,2,1024,1]{2,0,1,3:T(8,128)(2,1)}, u32[]{:S(2)}) copy-start(bf16[256,2,1024,1]{2,0,1,3:T(8,128)(2,1)} %constant.12) | copy-start | bytes 3145732
  36.9 102.5 %all-to-all-start = ((bf16[32,4,2,32,256]{4,3,2,1,0:T(8,128)(2,1)}), bf16[32,4,2,32,256]{4,3,2,1,0:T(8,128)(2,1)}, u32[]{:S(2)}, u32[]{:S(2)}) async-start(bf16[32,4,2,32,256]{4,3,2,1,0:T(8,128)(2,1)} %bitcast.36), calls=%async_computation | async-start | bytes 8388608 | tf_op jit(solution)/shard_map/all_to_all | solution.py:238
  139.4 3.9 %copy-start.6 = (s32[1024]{0:T(1024)S(1)}, s32[1024]{0:T(1024)}, u32[]{:S(2)}) copy-start(s32[1024]{0:T(1024)} %param.8) | copy-start | bytes 12292
  139.4 98.8 %all-to-all-start.2 = ((bf16[32,4,2,32,256]{4,3,2,1,0:T(8,128)(2,1)}), bf16[32,4,2,32,256]{4,3,2,1,0:T(8,128)(2,1)}, u32[]{:S(2)}, u32[]{:S(2)}) async-start(bf16[32,4,2,32,256]{4,3,2,1,0:T(8,128)(2,1)} %bitcast.35), calls=%async_computation.2 | async-start | bytes 8388608 | tf_op jit(solution)/shard_map/all_to_all | solution.py:238
  162.9 1.3 copy-start.3
  238.2 52.6 %all-to-all-start.1 = ((bf16[8,4,128,256]{3,2,1,0:T(8,128)(2,1)}), bf16[8,4,128,256]{3,2,1,0:T(8,128)(2,1)S(1)}, u32[]{:S(2)}, u32[]{:S(2)}) async-start(bf16[8,4,128,256]{3,2,1,0:T(8,128)(2,1)} %copy-done.3), calls=%async_computation.1 | async-start | bytes 4194304 | tf_op jit(solution)/shard_map/all_to_all | solution.py:240
  261.4 1.3 copy-start.2
  262.7 33.1 %copy-start.7 = (s32[64,32]{0,1:T(8,128)S(1)}, s32[64,32]{0,1:T(8,128)}, u32[]{:S(2)}) copy-start(s32[64,32]{0,1:T(8,128)} %param.9) | copy-start | bytes 24580
  290.8 1.3 copy-start
  292.1 52.6 %all-to-all-start.3 = ((bf16[8,4,128,256]{3,2,1,0:T(8,128)(2,1)}), bf16[8,4,128,256]{3,2,1,0:T(8,128)(2,1)S(1)}, u32[]{:S(2)}, u32[]{:S(2)}) async-start(bf16[8,4,128,256]{3,2,1,0:T(8,128)(2,1)} %copy-done.2), calls=%async_computation.3 | async-start | bytes 4194304 | tf_op jit(solution)/shard_map/all_to_all | solution.py:240
  295.9 1.6 copy-start.1
  305.8 1.3 copy-start.4
  344.7 1.6 copy-start.5
  346.3 17.2 %copy-start.8 = (bf16[8,2,4,128,256]{4,3,2,1,0:T(8,128)(2,1)S(1)}, bf16[8,2,4,128,256]{4,3,2,1,0:T(8,128)(2,1)}, u32[]{:S(2)}) copy-start(bf16[8,2,4,128,256]{4,3,2,1,0:T(8,128)(2,1)} %get-tuple-element.4) | copy-start | bytes 12582916
  363.7 2.2 copy-start.9
